TPU v7x, 32 devices: a whole 2x2x4 slice. The times are simulated.
32 devices in a mesh: blk: 8 (over z, x), tok: 4 (over y, core).
Axes of the slice: x: 2, y: 2, z: 4, core: 2. Of those that a mesh axis runs over, the one named last changes fastest.
Arguments:
- stream: bfloat16 [4096, 1664], P(('tok', 'blk'))
- queries: bfloat16 [4096, 1664], P(('tok', 'blk'))
- key_cache: bfloat16 [4096, 1664], P(('tok', 'blk'))
- value_cache: bfloat16 [4096, 1664], P(('tok', 'blk')), may hold values from -6 to 6
- segments: int32 [4096], P('tok'), may hold values from 63 to 4095, as said below
- stale_rows: int32 [384], P(('tok', 'blk')), may hold values from 0 to 4095, as said below
- owners: int32 [1024], P(('tok', 'blk')), may hold values from 0 to 3, as said below
- attn_gain: float32 [1664], replicated, may hold values from 0.1 to 1.9
- w_key: bfloat16 [1664, 1664], replicated, may hold values from -0.15625 to 0.15625
- key_bias: float32 [1664], replicated, may hold values from -3 to 3
- mlp_gain: float32 [1664], replicated, may hold values from 0.1 to 1.9
- w_fc: bfloat16 [1664, 8192], P(None, 'blk'), may hold values from -0.15625 to 0.15625
- b_fc: float32 [8192], P('blk'), may hold values from -3 to 3
- w_proj: bfloat16 [8192, 1664], P('blk'), may hold values from -0.125 to 0.125
- b_proj: float32 [1664], replicated, may hold values from -3 to 3
- merge_gain: float32 [1664], replicated, may hold values from 0.1 to 1.9
- w_merge: bfloat16 [1664, 1664], replicated, may hold values from -0.15625 to 0.15625
- b_merge: float32 [1664], replicated, may hold values from -3 to 3
Outputs:
- refreshed_keys: bfloat16 [4096, 1664], P(('tok', 'blk'))
- delivered: bfloat16 [4, 8, 128, 1664], P('tok', 'blk')
Inputs may be any that keep to these rules, and one draw needn't show every extreme that they name: `segments`: A segment's id is the index of its last row, so ids never fall; each segment has 4 to 128 rows, a multiple of 4, and lies inside one aligned block of 1024 rows; each such block begins with a segment of 64 rows followed by one of exactly 128 rows. `stale_rows`: Distinct; the aligned block of 128 rows of each device holds exactly 12 of them, all inside that block and listed on that device; row 0 and the last row are always listed. `owners`: all merged tokens of one segment (the segment of row 4 m for merged token m) have the same owner.
All inputs are finite; a program needn't handle non-finite values.
Results may differ from a plain program's by a relative error of at most 0.011.
Values may be sent and summed in bfloat16 or wider, within the bound.
A program may use at most 192 MiB of HBM per device.

v0:
```python
import jax
import jax.numpy as jnp
from jax import lax
from jax.sharding import PartitionSpec as P

HEADS = 16


def passed_along(block, axis, distance):
    devices = range(lax.axis_size(axis))
    route = [(i - distance, i) for i in devices if i - distance in devices]
    return lax.ppermute(block, axis, route)


def layer_norm(values, gain):
    center = values - jnp.mean(values, axis=-1, keepdims=True)
    spread = jnp.mean(center * center, axis=-1, keepdims=True)
    return center * lax.rsqrt(spread + 1e-06) * gain


def body(
    stream,
    queries,
    key_cache,
    value_cache,
    segments,
    stale_rows,
    owners,
    attn_gain,
    w_key,
    key_bias,
    mlp_gain,
    w_fc,
    b_fc,
    w_proj,
    b_proj,
    merge_gain,
    w_merge,
    b_merge,
):
    row_count = stream.shape[0]
    model_width = stream.shape[1]
    head_size = model_width // HEADS
    local_rows = stale_rows % row_count
    held = layer_norm(stream[local_rows].astype(jnp.float32), attn_gain).astype(jnp.bfloat16)
    fresh_keys = (jnp.dot(held, w_key, preferred_element_type=jnp.float32) + key_bias).astype(
        jnp.bfloat16
    )
    refreshed = key_cache.at[local_rows].set(fresh_keys)
    below = passed_along((refreshed, value_cache), "blk", 1)
    above = passed_along((refreshed, value_cache), "blk", -1)
    key_window = jnp.concatenate([below[0], refreshed, above[0]], axis=0).reshape(
        3 * row_count, HEADS, head_size
    )
    value_window = jnp.concatenate([below[1], value_cache, above[1]], axis=0).reshape(
        3 * row_count, HEADS, head_size
    )
    position = lax.axis_index("blk")
    minus_ones = jnp.full((row_count,), -1, jnp.int32)
    seg_padded = jnp.concatenate([minus_ones, segments, minus_ones], axis=0)
    key_seg = lax.dynamic_slice_in_dim(seg_padded, position * row_count, 3 * row_count, 0)
    query_seg = lax.dynamic_slice_in_dim(segments, position * row_count, row_count, 0)
    query_heads = queries.reshape(row_count, HEADS, head_size)
    scores = jnp.einsum(
        "qhd,khd->hqk", query_heads, key_window, preferred_element_type=jnp.float32
    ) * (1.0 / head_size**0.5)
    allowed = (query_seg[:, None] == key_seg[None, :])[None]
    scores = jnp.where(allowed, scores, -jnp.inf)
    top_score = jnp.max(scores, axis=-1, keepdims=True)
    weights = jnp.exp(scores - top_score)
    probs = (weights / jnp.sum(weights, axis=-1, keepdims=True)).astype(jnp.bfloat16)
    attended = jnp.einsum("hqk,khd->qhd", probs, value_window, preferred_element_type=jnp.float32)
    attended = attended.reshape(row_count, model_width).astype(jnp.bfloat16)
    mixed = stream.astype(jnp.float32) + attended.astype(jnp.float32)
    normed = layer_norm(mixed, mlp_gain).astype(jnp.bfloat16)
    group_units = jax.nn.gelu(
        jnp.dot(
            lax.all_gather(normed, "blk", axis=0, tiled=True),
            w_fc,
            preferred_element_type=jnp.float32,
        )
        + b_fc,
        approximate=False,
    ).astype(jnp.bfloat16)
    summed = lax.psum_scatter(
        jnp.dot(group_units, w_proj, preferred_element_type=jnp.float32).astype(jnp.bfloat16),
        "blk",
        scatter_dimension=0,
        tiled=True,
    ).astype(jnp.float32)
    pooled = jnp.mean((mixed + summed).reshape(row_count // 4, 4, model_width), axis=1) + b_proj
    merge_in = layer_norm(pooled, merge_gain).astype(jnp.bfloat16)
    merged = (jnp.dot(merge_in, w_merge, preferred_element_type=jnp.float32) + b_merge).astype(
        jnp.bfloat16
    )
    owner_count = lax.axis_size("tok")
    merged_rows = row_count // 4
    owner_hot = (owners[:, None] == jnp.arange(owner_count, dtype=jnp.int32)[None, :]).astype(
        jnp.int32
    )
    ranking = jnp.sum(jnp.cumsum(owner_hot, axis=0) * owner_hot, axis=-1) - 1
    selector = (
        owners[None, None, :] == jnp.arange(owner_count, dtype=jnp.int32)[:, None, None]
    ) & (ranking[None, None, :] == jnp.arange(merged_rows, dtype=jnp.int32)[None, :, None])
    outgoing = jnp.einsum(
        "osm,md->osd", selector.astype(jnp.bfloat16), merged, preferred_element_type=jnp.float32
    ).astype(jnp.bfloat16)
    arrived = lax.all_to_all(outgoing, "tok", split_axis=0, concat_axis=0, tiled=True)
    delivered = arrived.reshape(1, 1, owner_count * merged_rows, model_width)
    return (refreshed, delivered)


def solution(mesh):
    return jax.shard_map(
        body,
        mesh=mesh,
        in_specs=(
            P(("tok", "blk"), None),
            P(("tok", "blk"), None),
            P(("tok", "blk"), None),
            P(("tok", "blk"), None),
            P("tok"),
            P(("tok", "blk")),
            P(("tok", "blk")),
            P(),
            P(),
            P(),
            P(),
            P(None, "blk"),
            P("blk"),
            P("blk", None),
            P(),
            P(),
            P(),
            P(),
        ),
        out_specs=(P(("tok", "blk"), None), P("tok", "blk", None, None)),
        check_vma=False,
    )
```

profile of v0, /device:TPU:27, one launch (start us, length us, event | category | flops | bytes accessed | tf_op | source)
XLA Modules:
  0.0 272.4 jit_solution(3619419935331788393)
XLA Ops:
  7.2 0.0 copy-start
  7.2 0.0 all-gather.2.cloned.1.call-start
  7.2 1.9 copy.39
  9.2 0.7 compare_select_fusion
  9.9 1.7 gather_fusion
  11.6 0.1 convert_reduce_fusion
  11.7 0.2 fusion.60
  11.9 3.4 %fusion.14 = bf16[12,1664]{1,0:T(8,128)(2,1)S(1)} fusion(bf16[1664,1664]{1,0:T(8,128)(2,1)} %param.26, bf16[12,1664]{1,0:T(8,128)(2,1)S(1)} %gather_fusion, f32[1664]{0:T(1024)} %param.27, f32[1664]{0:T(1024)} %param.25, f32[12]{0:T(128)S(1)} %add_rsqrt_fusion.2, f32[12]{0:T(128)S(1)} %broadcast_multiply_fusion.2), kind=kOutput, calls=%fused_computation.32 | convolution fusion | flops 66593280 | bytes 5631072 | tf_op jit(solution)/shard_map/dot_general | solution.py:46
  15.3 2.5 scatter_fusion
  17.8 1.3 collective-permute-start.2
  19.1 4.7 %collective-permute-start.3 = (bf16[128,1664]{1,0:T(8,128)(2,1)}, bf16[128,1664]{1,0:T(8,128)(2,1)}, u32[]{:S(2)}, u32[]{:S(2)}) collective-permute-start(bf16[128,1664]{1,0:T(8,128)(2,1)} %scatter_fusion), channel_id=1, source_target_pairs={{4,0},{8,4},{12,8},{16,12},{20,16},{24,20},{28,24},{5,1},{9,5},{13... | collective-permute-start | bytes 1277960 | tf_op jit(solution)/shard_map/ppermute | solution.py:12
  23.9 1.3 collective-permute-start
  25.2 4.8 %collective-permute-start.1 = (bf16[128,1664]{1,0:T(8,128)(2,1)}, bf16[128,1664]{1,0:T(8,128)(2,1)}, u32[]{:S(2)}, u32[]{:S(2)}) collective-permute-start(bf16[128,1664]{1,0:T(8,128)(2,1)} %param.21), channel_id=1, source_target_pairs={{4,0},{8,4},{12,8},{16,12},{20,16},{24,20},{28,24},{5,1},{9,5},{13... | collective-permute-start | bytes 1277960 | tf_op jit(solution)/shard_map/ppermute | solution.py:12
  29.9 2.0 copy.32
  31.9 0.1 dynamic_slice.6
  32.0 0.1 fusion.84
  32.1 0.1 broadcast_compare_fusion
  32.2 0.0 collective-permute-done.2
  32.2 16.8 %collective-permute-done.3 = bf16[128,1664]{1,0:T(8,128)(2,1)} collective-permute-done((bf16[128,1664]{1,0:T(8,128)(2,1)}, bf16[128,1664]{1,0:T(8,128)(2,1)}, u32[]{:S(2)}, u32[]{:S(2)}) %collective-permute-start.3) | collective-permute-done | bytes 426016 | tf_op jit(solution)/shard_map/ppermute | solution.py:12
  49.0 2.4 pad_maximum_fusion.1
  51.4 2.5 copy.31
  53.8 4.3 %collective-permute-done.1 = bf16[128,1664]{1,0:T(8,128)(2,1)} collective-permute-done((bf16[128,1664]{1,0:T(8,128)(2,1)}, bf16[128,1664]{1,0:T(8,128)(2,1)}, u32[]{:S(2)}, u32[]{:S(2)}) %collective-permute-start.1) | collective-permute-done | bytes 426016 | tf_op jit(solution)/shard_map/ppermute | solution.py:12
  58.1 2.4 pad_maximum_fusion
  60.5 2.5 copy.30
  63.0 4.3 %fusion.120 = (f32[16,128]{1,0:T(8,128)S(1)}, f32[16,128,384]{1,2,0:T(8,128)}) fusion(pred[128,384]{0,1:T(8,128)(4,1)S(1)} %broadcast_compare_fusion, bf16[384,16,104]{0,2,1:T(8,128)(2,1)} %bitcast.33, bf16[128,16,104]{0,2,1:T(8,128)(2,1)} %bitcast.36), kind=kOutput, calls=%fused_computation.159 | convolution fusion | flops 166723968 | bytes 4907008 | tf_op jit(solution)/shard_map/sub | solution.py:70
  67.3 3.8 %fusion.54 = f32[16,104,128]{2,1,0:T(8,128)} fusion(bf16[384,16,104]{0,2,1:T(8,128)(2,1)} %bitcast.34, f32[16,128,384]{1,2,0:T(8,128)} %get-tuple-element.3, f32[16,128]{1,0:T(8,128)S(1)} %get-tuple-element.2), kind=kOutput, calls=%fused_computation.72 | convolution fusion | flops 165576704 | bytes 5283840 | tf_op jit(solution)/shard_map/hqk,khd->qhd/dot_general | solution.py:72
  71.1 2.4 copy.34
  73.4 1.4 fusion.75
  74.9 1.5 multiply_reduce_fusion
  76.4 2.2 multiply_convert_fusion
  78.6 0.0 all-gather.2.cloned.1.call-update
  78.7 0.0 copy-start.6
  78.7 0.2 reduce-scatter.2.cloned.1.call-start
  78.9 62.9 %all-gather.2.cloned.1.call-done = bf16[1024,1664]{1,0:T(8,128)(2,1)} async-done(((bf16[128,1664]{1,0:T(8,128)(2,1)}), bf16[1024,1664]{1,0:T(8,128)(2,1)}) %all-gather.2.cloned.1.call-update) | async-done | bytes 3407888 | tf_op jit(solution)/shard_map/all_gather | solution.py:78
  141.8 20.3 %convolution_convert_fusion = bf16[1024,1664]{1,0:T(8,128)(2,1)} fusion(bf16[1024,1664]{1,0:T(8,128)(2,1)S(1)} %copy-done, bf16[1024,1664]{1,0:T(8,128)(2,1)} %all-gather.2.cloned.1.call-done, bf16[1664,1024]{1,0:T(8,128)(2,1)} %param.29, f32[1024]{0:T(1024)S(1)} %copy-done.7), kind=kOutput, calls=%fused_computation.22 | convolution fusion | flops 7050231808 | bytes 13635584 | tf_op jit(solution)/shard_map/dot_general | solution.py:86
  162.1 0.0 reduce-scatter.2.cloned.1.call-update
  162.2 0.1 fusion.82
  162.2 0.1 reduce_window_sum.11
  162.3 0.2 select_reduce_fusion
  162.5 76.5 %reduce-scatter.2.cloned.1.call-done = bf16[128,1664]{1,0:T(8,128)(2,1)} async-done(((bf16[1024,1664]{1,0:T(8,128)(2,1)}), bf16[128,1664]{1,0:T(8,128)(2,1)}) %reduce-scatter.2.cloned.1.call-update) | async-done | bytes 426000 | tf_op jit(solution)/shard_map/reduce_scatter | solution.py:85
  239.0 2.4 convert_add_fusion
  241.4 2.3 reshape.147
  243.7 2.3 reduce_sum.87
  246.1 1.1 fusion.55
  247.2 1.1 multiply_reduce_fusion.1
  248.3 4.7 %convolution_convert_fusion.1 = bf16[4,32,1664]{2,1,0:T(8,128)(2,1)} fusion(bf16[1664,1664]{1,0:T(8,128)(2,1)} %param.34, f32[32,1664]{1,0:T(8,128)} %reduce_sum.87, f32[1664]{0:T(1024)S(1)} %copy-done.3, f32[1664]{0:T(1024)S(1)} %copy-done.4, f32[32]{0:T(128)S(1)} %add_rsqrt_fusion, f32[32]{0:T(128)S(1)} %broadcast_multiply_fusion, ...), kind=kOutput, calls=%fused_computation.26 | convolution fusion | flops 191483904 | bytes 6198144 | tf_op jit(solution)/shard_map/osm,md->osd/dot_general | solution.py:105
  253.0 11.8 %all_to_all.5 = bf16[4,32,1664]{2,1,0:T(8,128)(2,1)S(1)} all-to-all(bf16[4,32,1664]{2,1,0:T(8,128)(2,1)} %convolution_convert_fusion.1), channel_id=1, replica_groups=mesh['blk'=8,'tok'=4] {'tok'}, dimensions={0} | all-to-all | bytes 851968 | tf_op jit(solution)/shard_map/all_to_all | solution.py:108
  264.8 0.8 copy.40
  (26 shorter events, 0.1 us)
Async XLA Ops:
  7.2 134.7 %copy-start = (bf16[1024,1664]{1,0:T(8,128)(2,1)S(1)}, bf16[1024,1664]{1,0:T(8,128)(2,1)}, u32[]{:S(2)}) copy-start(bf16[1024,1664]{1,0:T(8,128)(2,1)} %param.31) | copy-start | bytes 10223620
  7.2 134.6 %all-gather.2.cloned.1.call-start = ((), (), s32[]{:S(2)}) async-start(), calls=%async_computation.2 | async-start | bytes 3833856 | tf_op jit(solution)/shard_map/all_gather | solution.py:78
  9.2 22.7 %copy-start.5 = (s32[1024]{0:T(1024)S(1)}, s32[1024]{0:T(1024)}, u32[]{:S(2)}) copy-start(s32[1024]{0:T(1024)} %param.22) | copy-start | bytes 12292
  17.8 14.4 %collective-permute-start.2 = (bf16[128,1664]{1,0:T(8,128)(2,1)}, bf16[128,1664]{1,0:T(8,128)(2,1)}, u32[]{:S(2)}, u32[]{:S(2)}) collective-permute-start(bf16[128,1664]{1,0:T(8,128)(2,1)} %scatter_fusion), channel_id=1, source_target_pairs={{0,4},{4,8},{8,12},{12,16},{16,20},{20,24},{24,28},{1,5},{5,9},{9,... | collective-permute-start | bytes 1277960 | tf_op jit(solution)/shard_map/ppermute | solution.py:12
  19.1 29.9 %collective-permute-start.3 = (bf16[128,1664]{1,0:T(8,128)(2,1)}, bf16[128,1664]{1,0:T(8,128)(2,1)}, u32[]{:S(2)}, u32[]{:S(2)}) collective-permute-start(bf16[128,1664]{1,0:T(8,128)(2,1)} %scatter_fusion), channel_id=1, source_target_pairs={{4,0},{8,4},{12,8},{16,12},{20,16},{24,20},{28,24},{5,1},{9,5},{13... | collective-permute-start | bytes 1277960 | tf_op jit(solution)/shard_map/ppermute | solution.py:12
  23.9 30.0 %collective-permute-start = (bf16[128,1664]{1,0:T(8,128)(2,1)}, bf16[128,1664]{1,0:T(8,128)(2,1)}, u32[]{:S(2)}, u32[]{:S(2)}) collective-permute-start(bf16[128,1664]{1,0:T(8,128)(2,1)} %param.21), channel_id=1, source_target_pairs={{0,4},{4,8},{8,12},{12,16},{16,20},{20,24},{24,28},{1,5},{5,9},{9,... | collective-permute-start | bytes 1277960 | tf_op jit(solution)/shard_map/ppermute | solution.py:12
  25.2 33.0 %collective-permute-start.1 = (bf16[128,1664]{1,0:T(8,128)(2,1)}, bf16[128,1664]{1,0:T(8,128)(2,1)}, u32[]{:S(2)}, u32[]{:S(2)}) collective-permute-start(bf16[128,1664]{1,0:T(8,128)(2,1)} %param.21), channel_id=1, source_target_pairs={{4,0},{8,4},{12,8},{16,12},{20,16},{24,20},{28,24},{5,1},{9,5},{13... | collective-permute-start | bytes 1277960 | tf_op jit(solution)/shard_map/ppermute | solution.py:12
  71.1 5.3 %copy-start.2 = (f32[1664]{0:T(1024)S(1)}, f32[1664]{0:T(1024)}, u32[]{:S(2)}) copy-start(f32[1664]{0:T(1024)} %param.28) | copy-start | bytes 19972
  71.1 70.8 %copy-start.7 = (f32[1024]{0:T(1024)S(1)}, f32[1024]{0:T(1024)}, u32[]{:S(2)}) copy-start(f32[1024]{0:T(1024)} %param.30) | copy-start | bytes 12292
  78.7 83.5 %copy-start.6 = (s32[32]{0:T(128)S(1)}, s32[32]{0:T(128)}, u32[]{:S(2)}) copy-start(s32[32]{0:T(128)} %param.24) | copy-start | bytes 388
  78.7 160.4 %reduce-scatter.2.cloned.1.call-start = ((), (), s32[]{:S(2)}) async-start(), calls=%async_computation.3 | async-start | bytes 3833856 | tf_op jit(solution)/shard_map/reduce_scatter | solution.py:85
  162.1 84.0 %copy-start.1 = (f32[1664]{0:T(1024)S(1)}, f32[1664]{0:T(1024)}, u32[]{:S(2)}) copy-start(f32[1664]{0:T(1024)} %param.32) | copy-start | bytes 19972
  162.1 86.2 %copy-start.3 = (f32[1664]{0:T(1024)S(1)}, f32[1664]{0:T(1024)}, u32[]{:S(2)}) copy-start(f32[1664]{0:T(1024)} %param.35) | copy-start | bytes 19972
  162.1 86.2 %copy-start.4 = (f32[1664]{0:T(1024)S(1)}, f32[1664]{0:T(1024)}, u32[]{:S(2)}) copy-start(f32[1664]{0:T(1024)} %param.33) | copy-start | bytes 19972
Sparse Core Ops, SparseCore 0:
  78.8 63.0 all-gather.1
  162.3 76.7 reduce-scatter.1
where the time goes:
time: 276 us; the launch traced here: 272 us
  waiting for transfers between devices  161 us (58%)
  matrix products  36.5 us (13%)
  local copies, waits for them, and re-layouts  18.6 us (7%)
  other arithmetic  18.5 us (7%)
  between operations  14.2 us (5%)
  starting transfers between devices  12.3 us (4%)
  blocking collectives  11.8 us (4%)
    reduce_scatter x1, waiting for transfers between devices, body(): lax.psum_scatter(jnp.dot(group_units, w_proj, preferred_element_type=jnp....  76.5 us
    all_gather x1, waiting for transfers between devices, body(): lax.all_gather(normed, 'blk', axis=0, tiled=True)  62.9 us
    ppermute x4, waiting for transfers between devices, passed_along(): return lax.ppermute(block, axis, route)  21 us
    dot_general x1, matrix products, body(): jnp.dot(group_units, w_proj, preferred_element_type=jnp.float32)  20.3 us
    ppermute x4, starting transfers between devices, passed_along(): return lax.ppermute(block, axis, route)  12.1 us
    all_to_all x1, blocking collectives, body(): lax.all_to_all(outgoing, 'tok', split_axis=0, concat_axis=0, tiled=True)  11.8 us
  transfers between devices with their start and end apart: 6, of which 4 were waited for; matrix products, arithmetic and copies ran while one was open for 3% of the time, Pallas kernels for 0%

commit v1 on v0

--- a/solution.py
+++ b/solution.py
@@ -82,13 +82,17 @@
         + b_fc,
         approximate=False,
     ).astype(jnp.bfloat16)
+    pooled_units = jnp.sum(
+        group_units.astype(jnp.float32).reshape(group_units.shape[0] // 4, 4, -1), axis=1
+    ).astype(jnp.bfloat16)
     summed = lax.psum_scatter(
-        jnp.dot(group_units, w_proj, preferred_element_type=jnp.float32).astype(jnp.bfloat16),
+        jnp.dot(pooled_units, w_proj, preferred_element_type=jnp.float32).astype(jnp.bfloat16),
         "blk",
         scatter_dimension=0,
         tiled=True,
     ).astype(jnp.float32)
-    pooled = jnp.mean((mixed + summed).reshape(row_count // 4, 4, model_width), axis=1) + b_proj
+    own = jnp.sum(mixed.reshape(row_count // 4, 4, model_width), axis=1)
+    pooled = (own + summed) * 0.25 + b_proj
     merge_in = layer_norm(pooled, merge_gain).astype(jnp.bfloat16)
     merged = (jnp.dot(merge_in, w_merge, preferred_element_type=jnp.float32) + b_merge).astype(
         jnp.bfloat16

time: 276 us -> 253 us (0.917)
  waiting for transfers between devices: 161 us -> 133 us
  local copies, waits for them, and re-layouts: 18.6 us -> 23.4 us
    reduce_scatter x1, waiting for transfers between devices: 76.5 us -> 55.6 us  [body(): lax.psum_scatter(jnp.dot(pooled_units, w_proj, preferred_element_type=jnp...]
    ppermute x4, waiting for transfers between devices: 21 us -> 12.3 us  [passed_along(): return lax.ppermute(block, axis, route)]
    reduce_sum x1 -> x2, other arithmetic: 2.34 us -> 7.28 us  [the longest x1 4.94 us: body(): jnp.sum(group_units.astype(jnp.float32).reshape(group_units.shape[0] // 4...]
    reshape x1 -> x2, local copies, waits for them, and re-layouts: 2.31 us -> 6.43 us  [the longest x1 4.11 us: body(): group_units.astype(jnp.float32).reshape(group_units.shape[0] // 4, 4, -1)]
    dot_general x1 -> x2, matrix products: 20.3 us -> 19.4 us  [the longest x1 15.2 us: body(): jnp.dot(lax.all_gather(normed, 'blk', axis=0, tiled=True), w_fc, preferre...]
  transfers between devices with their start and end apart: 6 -> 6, of which waited for: 4 -> 3; matrix products, arithmetic and copies ran while one was open for 3% -> 8% of each run, Pallas kernels for 0% -> 0%
where the time goes in v1:
time: 253 us; the launch traced here: 248 us
  waiting for transfers between devices  133 us (53%)
  matrix products  35.7 us (14%)
  local copies, waits for them, and re-layouts  23.4 us (9%)
  other arithmetic  18.6 us (7%)
  between operations  14.2 us (6%)
  blocking collectives  13 us (5%)
  starting transfers between devices  10.6 us (4%)
    all_gather x1, waiting for transfers between devices, body(): lax.all_gather(normed, 'blk', axis=0, tiled=True)  64.8 us
    reduce_scatter x1, waiting for transfers between devices, body(): lax.psum_scatter(jnp.dot(pooled_units, w_proj, preferred_element_type=jnp...  55.6 us
    dot_general x1, matrix products, body(): jnp.dot(lax.all_gather(normed, 'blk', axis=0, tiled=True), w_fc, preferre...  15.2 us
    all_to_all x1, blocking collectives, body(): lax.all_to_all(outgoing, 'tok', split_axis=0, concat_axis=0, tiled=True)  13 us
    ppermute x4, waiting for transfers between devices, passed_along(): return lax.ppermute(block, axis, route)  12.3 us
    ppermute x4, starting transfers between devices, passed_along(): return lax.ppermute(block, axis, route)  10.4 us
    unnamed x21, local copies, waits for them, and re-layouts  5.39 us
  transfers between devices with their start and end apart: 6, of which 3 were waited for; matrix products, arithmetic and copies ran while one was open for 8% of the time, Pallas kernels for 0%

profile of v1, /device:TPU:27, one launch (start us, length us, event | category | flops | bytes accessed | tf_op | source)
XLA Modules:
  0.0 248.2 jit_solution(5978828190871113116)
XLA Ops:
  7.2 0.0 copy-start
  7.2 0.0 all-gather.2.cloned.1.call-start
  7.2 1.9 copy.34
  9.2 3.0 %collective-permute-start.1 = (bf16[128,1664]{1,0:T(8,128)(2,1)}, bf16[128,1664]{1,0:T(8,128)(2,1)}, u32[]{:S(2)}, u32[]{:S(2)}) collective-permute-start(bf16[128,1664]{1,0:T(8,128)(2,1)} %param.21), channel_id=1, source_target_pairs={{4,0},{8,4},{12,8},{16,12},{20,16},{24,20},{28,24},{5,1},{9,5},{13... | collective-permute-start | bytes 1277960 | tf_op jit(solution)/shard_map/ppermute | solution.py:12
  12.2 1.3 collective-permute-start
  13.5 0.7 compare_select_fusion
  14.2 1.7 gather_fusion
  15.9 0.1 convert_reduce_fusion
  16.0 0.2 fusion.25
  16.2 3.4 %fusion.14 = bf16[12,1664]{1,0:T(8,128)(2,1)S(1)} fusion(bf16[1664,1664]{1,0:T(8,128)(2,1)} %param.26, bf16[12,1664]{1,0:T(8,128)(2,1)S(1)} %gather_fusion, f32[1664]{0:T(1024)} %param.27, f32[1664]{0:T(1024)} %param.25, f32[12]{0:T(128)S(1)} %add_rsqrt_fusion.2, f32[12]{0:T(128)S(1)} %broadcast_multiply_fusion.2), kind=kOutput, calls=%fused_computation.32 | convolution fusion | flops 66593280 | bytes 5631072 | tf_op jit(solution)/shard_map/dot_general | solution.py:46
  19.7 2.5 %scatter_fusion = bf16[128,1664]{1,0:T(8,128)(2,1)} fusion(bf16[128,1664]{1,0:T(8,128)(2,1)} %copy.34, s32[12]{0:T(128)S(1)} %compare_select_fusion, bf16[12,1664]{1,0:T(8,128)(2,1)S(1)} %fusion.14), kind=kCustom, calls=%fused_computation.1 | custom fusion | bytes 119856 | tf_op jit(solution)/shard_map/scatter | solution.py:49
  22.1 4.8 %collective-permute-start.3 = (bf16[128,1664]{1,0:T(8,128)(2,1)}, bf16[128,1664]{1,0:T(8,128)(2,1)}, u32[]{:S(2)}, u32[]{:S(2)}) collective-permute-start(bf16[128,1664]{1,0:T(8,128)(2,1)} %scatter_fusion), channel_id=1, source_target_pairs={{4,0},{8,4},{12,8},{16,12},{20,16},{24,20},{28,24},{5,1},{9,5},{13... | collective-permute-start | bytes 1277960 | tf_op jit(solution)/shard_map/ppermute | solution.py:12
  26.9 1.3 collective-permute-start.2
  28.2 2.0 copy.27
  30.2 0.1 dynamic_slice.6
  30.2 0.1 fusion.45
  30.3 0.1 broadcast_compare_fusion
  30.5 2.4 pad_maximum_fusion
  32.9 2.5 copy.25
  35.4 12.3 %collective-permute-done.3 = bf16[128,1664]{1,0:T(8,128)(2,1)} collective-permute-done((bf16[128,1664]{1,0:T(8,128)(2,1)}, bf16[128,1664]{1,0:T(8,128)(2,1)}, u32[]{:S(2)}, u32[]{:S(2)}) %collective-permute-start.3) | collective-permute-done | bytes 426016 | tf_op jit(solution)/shard_map/ppermute | solution.py:12
  47.6 2.4 pad_maximum_fusion.1
  50.0 2.5 copy.26
  52.5 4.3 %fusion.52 = (f32[16,128]{1,0:T(8,128)S(1)}, f32[16,128,384]{1,2,0:T(8,128)}) fusion(pred[128,384]{0,1:T(8,128)(4,1)S(1)} %broadcast_compare_fusion, bf16[384,16,104]{0,2,1:T(8,128)(2,1)} %bitcast.35, bf16[128,16,104]{0,2,1:T(8,128)(2,1)} %bitcast.37), kind=kOutput, calls=%fused_computation.94 | convolution fusion | flops 166723968 | bytes 4907008 | tf_op jit(solution)/shard_map/sub | solution.py:70
  56.8 3.8 %fusion.20 = f32[16,104,128]{2,1,0:T(8,128)} fusion(bf16[384,16,104]{0,2,1:T(8,128)(2,1)} %bitcast.34, f32[16,128,384]{1,2,0:T(8,128)} %get-tuple-element.5, f32[16,128]{1,0:T(8,128)S(1)} %get-tuple-element.4), kind=kOutput, calls=%fused_computation.40 | convolution fusion | flops 165576704 | bytes 5283840 | tf_op jit(solution)/shard_map/hqk,khd->qhd/dot_general | solution.py:72
  60.6 2.4 copy.29
  63.0 1.4 fusion.51
  64.4 0.2 multiply_reduce_fusion
  64.7 0.7 copy-done.1
  65.4 0.9 multiply_convert_fusion
  66.3 0.0 all-gather.2.cloned.1.call-update
  66.3 0.2 reduce-scatter.2.cloned.1.call-start
  66.5 64.8 %all-gather.2.cloned.1.call-done = bf16[1024,1664]{1,0:T(8,128)(2,1)} async-done(((bf16[128,1664]{1,0:T(8,128)(2,1)}), bf16[1024,1664]{1,0:T(8,128)(2,1)}) %all-gather.2.cloned.1.call-update) | async-done | bytes 3407888 | tf_op jit(solution)/shard_map/all_gather | solution.py:78
  131.4 15.2 %fusion.3 = bf16[1024,1024]{1,0:T(8,128)(2,1)} fusion(f32[1024]{0:T(1024)S(1)} %copy-done.8, bf16[1024,1664]{1,0:T(8,128)(2,1)} %all-gather.2.cloned.1.call-done, bf16[1664,1024]{1,0:T(8,128)(2,1)S(1)} %copy-done), kind=kOutput, calls=%fused_computation.6 | convolution fusion | flops 3558866944 | bytes 8916992 | tf_op jit(solution)/shard_map/dot_general | solution.py:77
  146.5 4.1 %reshape.154 = bf16[256,4,1024]{2,1,0:T(4,128)(2,1)} reshape(bf16[1024,1024]{1,0:T(8,128)(2,1)} %fusion.3) | data formatting | bytes 4194304 | tf_op jit(solution)/shard_map/reshape | solution.py:86
  150.7 4.9 %reduce = bf16[256,1024]{1,0:T(8,128)(2,1)} reduce(bf16[256,4,1024]{2,1,0:T(4,128)(2,1)} %reshape.154, bf16[]{:T(256)} %constant.118), dimensions={1}, to_apply=%region_10.11.clone | reduce | flops 786432 | bytes 2621442 | tf_op jit(solution)/shard_map/reduce_sum | solution.py:85
  155.6 4.2 %convolution_convert_fusion = bf16[256,1664]{1,0:T(8,128)(2,1)} fusion(bf16[256,1024]{1,0:T(8,128)(2,1)} %reduce, bf16[1024,1664]{1,0:T(8,128)(2,1)} %param.31), kind=kOutput, calls=%fused_computation.25 | convolution fusion | flops 872841216 | bytes 4784128 | tf_op jit(solution)/shard_map/dot_general | solution.py:89
  159.8 0.0 reduce-scatter.2.cloned.1.call-update
  159.8 0.1 fusion.43
  159.9 0.1 reduce_window_sum.11
  160.0 0.2 select_reduce_fusion
  160.2 2.3 reshape.153
  162.5 2.3 reduce_sum.94
  164.8 55.6 %reduce-scatter.2.cloned.1.call-done = bf16[32,1664]{1,0:T(8,128)(2,1)} async-done(((bf16[256,1664]{1,0:T(8,128)(2,1)}), bf16[32,1664]{1,0:T(8,128)(2,1)}) %reduce-scatter.2.cloned.1.call-update) | async-done | bytes 106512 | tf_op jit(solution)/shard_map/reduce_scatter | solution.py:88
  220.5 1.1 fusion.42
  221.6 1.2 multiply_reduce_fusion.1
  222.9 4.8 %convolution_convert_fusion.1 = bf16[4,32,1664]{2,1,0:T(8,128)(2,1)} fusion(bf16[1664,1664]{1,0:T(8,128)(2,1)} %param.34, f32[1664]{0:T(1024)S(1)} %copy-done.4, f32[1664]{0:T(1024)S(1)} %copy-done.5, f32[32]{0:T(128)S(1)} %add_rsqrt_fusion, f32[32]{0:T(128)S(1)} %broadcast_multiply_fusion, pred[32,32]{1,0:T(8,128)(4,1)S(1)} %iota_compare_fusion, ...), kind=kOutput, calls=%fused_computation.26 | convolution fusion | flops 191590400 | bytes 6304640 | tf_op jit(solution)/shard_map/osm,md->osd/dot_general | solution.py:109
  227.6 13.0 %all_to_all.5 = bf16[4,32,1664]{2,1,0:T(8,128)(2,1)S(1)} all-to-all(bf16[4,32,1664]{2,1,0:T(8,128)(2,1)} %convolution_convert_fusion.1), channel_id=1, replica_groups=mesh['blk'=8,'tok'=4] {'tok'}, dimensions={0} | all-to-all | bytes 851968 | tf_op jit(solution)/shard_map/all_to_all | solution.py:112
  240.6 0.8 copy.35
  (30 shorter events, 0.1 us)
Async XLA Ops:
  7.2 124.2 %copy-start = (bf16[1664,1024]{1,0:T(8,128)(2,1)S(1)}, bf16[1664,1024]{1,0:T(8,128)(2,1)}, u32[]{:S(2)}) copy-start(bf16[1664,1024]{1,0:T(8,128)(2,1)} %param.29) | copy-start | bytes 10223620
  7.2 124.2 %all-gather.2.cloned.1.call-start = ((), (), s32[]{:S(2)}) async-start(), calls=%async_computation.2 | async-start | bytes 3833856 | tf_op jit(solution)/shard_map/all_gather | solution.py:78
  9.2 21.0 %copy-start.6 = (s32[1024]{0:T(1024)S(1)}, s32[1024]{0:T(1024)}, u32[]{:S(2)}) copy-start(s32[1024]{0:T(1024)} %param.22) | copy-start | bytes 12292
  9.2 21.3 %collective-permute-start.1 = (bf16[128,1664]{1,0:T(8,128)(2,1)}, bf16[128,1664]{1,0:T(8,128)(2,1)}, u32[]{:S(2)}, u32[]{:S(2)}) collective-permute-start(bf16[128,1664]{1,0:T(8,128)(2,1)} %param.21), channel_id=1, source_target_pairs={{4,0},{8,4},{12,8},{16,12},{20,16},{24,20},{28,24},{5,1},{9,5},{13... | collective-permute-start | bytes 1277960 | tf_op jit(solution)/shard_map/ppermute | solution.py:12
  12.2 18.3 %collective-permute-start = (bf16[128,1664]{1,0:T(8,128)(2,1)}, bf16[128,1664]{1,0:T(8,128)(2,1)}, u32[]{:S(2)}, u32[]{:S(2)}) collective-permute-start(bf16[128,1664]{1,0:T(8,128)(2,1)} %param.21), channel_id=1, source_target_pairs={{0,4},{4,8},{8,12},{12,16},{16,20},{20,24},{24,28},{1,5},{5,9},{9,... | collective-permute-start | bytes 1277960 | tf_op jit(solution)/shard_map/ppermute | solution.py:12
  22.1 25.5 %collective-permute-start.3 = (bf16[128,1664]{1,0:T(8,128)(2,1)}, bf16[128,1664]{1,0:T(8,128)(2,1)}, u32[]{:S(2)}, u32[]{:S(2)}) collective-permute-start(bf16[128,1664]{1,0:T(8,128)(2,1)} %scatter_fusion), channel_id=1, source_target_pairs={{4,0},{8,4},{12,8},{16,12},{20,16},{24,20},{28,24},{5,1},{9,5},{13... | collective-permute-start | bytes 1277960 | tf_op jit(solution)/shard_map/ppermute | solution.py:12
  26.9 20.7 %collective-permute-start.2 = (bf16[128,1664]{1,0:T(8,128)(2,1)}, bf16[128,1664]{1,0:T(8,128)(2,1)}, u32[]{:S(2)}, u32[]{:S(2)}) collective-permute-start(bf16[128,1664]{1,0:T(8,128)(2,1)} %scatter_fusion), channel_id=1, source_target_pairs={{0,4},{4,8},{8,12},{12,16},{16,20},{20,24},{24,28},{1,5},{5,9},{9,... | collective-permute-start | bytes 1277960 | tf_op jit(solution)/shard_map/ppermute | solution.py:12
  60.6 4.8 %copy-start.3 = (f32[1664]{0:T(1024)S(1)}, f32[1664]{0:T(1024)}, u32[]{:S(2)}) copy-start(f32[1664]{0:T(1024)} %param.28) | copy-start | bytes 19972
  60.6 70.8 %copy-start.8 = (f32[1024]{0:T(1024)S(1)}, f32[1024]{0:T(1024)}, u32[]{:S(2)}) copy-start(f32[1024]{0:T(1024)} %param.30) | copy-start | bytes 12292
  64.4 0.9 copy-start.1
  66.3 154.1 %reduce-scatter.2.cloned.1.call-start = ((), (), s32[]{:S(2)}) async-start(), calls=%async_computation.3 | async-start | bytes 958464 | tf_op jit(solution)/shard_map/reduce_scatter | solution.py:88
  150.7 9.2 %copy-start.7 = (s32[32]{0:T(128)S(1)}, s32[32]{0:T(128)}, u32[]{:S(2)}) copy-start(s32[32]{0:T(128)} %param.24) | copy-start | bytes 388
  155.6 64.9 %copy-start.2 = (f32[1664]{0:T(1024)S(1)}, f32[1664]{0:T(1024)}, u32[]{:S(2)}) copy-start(f32[1664]{0:T(1024)} %param.32) | copy-start | bytes 19972
  155.6 67.2 %copy-start.4 = (f32[1664]{0:T(1024)S(1)}, f32[1664]{0:T(1024)}, u32[]{:S(2)}) copy-start(f32[1664]{0:T(1024)} %param.35) | copy-start | bytes 19972
  155.6 67.3 %copy-start.5 = (f32[1664]{0:T(1024)S(1)}, f32[1664]{0:T(1024)}, u32[]{:S(2)}) copy-start(f32[1664]{0:T(1024)} %param.33) | copy-start | bytes 19972
Sparse Core Ops, SparseCore 0:
  66.4 64.8 all-gather.1
  159.9 60.4 reduce-scatter.1
